TPU v7x, 128 devices: a whole 4x4x4 slice. The times are simulated.
128 devices in a mesh: ctx: 32 (over z_lo, x, y), head: 4 (over z_hi, core).
Axes of the slice: x: 4, y: 4, z: 4 (z_hi: 2, z_lo: 2; z = z_hi * 2 + z_lo), core: 2. Of those that a mesh axis runs over, the one named last changes fastest.
Arguments:
- queries: bfloat16 [4096, 12288], P('ctx', 'head'), may hold values from -230 to 230
- latents: bfloat16 [576, 4096], P(None, 'ctx'), may hold values from -6 to 6
- w_key: bfloat16 [64, 128, 512], P('head'), may hold values from -0.5 to 0.5
- w_value: bfloat16 [64, 512, 128], P('head'), may hold values from -0.25 to 0.25
- w_out: bfloat16 [8192, 3584], P('head'), may hold values from -0.0625 to 0.0625
- block_order: int32 [32], replicated, may hold values from 0 to 31, each once
Outputs:
- attended: bfloat16 [3584, 4096], P('head', 'ctx')
All inputs are finite; a program needn't handle non-finite values.
Results may differ from a plain program's by a relative error of at most 0.017.
Values may be sent and summed in bfloat16 or wider, within the bound.
A program may use at most 192 MiB of HBM per device.

v0:
```python
import math

import jax
import jax.numpy as jnp
from jax import lax
from jax.sharding import PartitionSpec as P

NOPE = 128
R = 64
C = 512
V = 128


NEG = -1e30


def from_behind(value, axis, steps):
    count = lax.axis_size(axis)
    pairs = [(source, (source + steps) % count) for source in range(count)]
    return lax.ppermute(value, axis, pairs)


def pick_entries(table, index):
    count = table.shape[0]
    hits = index[:, None] == jnp.arange(count, dtype=jnp.int32)[None, :]
    return jnp.sum(jnp.where(hits, table[None, :], 0), axis=1)


def shards(queries, latents, w_key, w_value, w_out, block_order):
    span = queries.shape[0]
    heads = w_key.shape[0]
    grouped = queries.reshape(span, heads, NOPE + R)
    absorbed = jnp.einsum(
        "thn,hnc->htc", grouped[:, :, :NOPE], w_key, preferred_element_type=jnp.float32
    ).astype(jnp.bfloat16)
    rope_part = jnp.transpose(grouped[:, :, NOPE:], (1, 0, 2))
    query_cat = jnp.concatenate([absorbed, rope_part], axis=2).reshape(heads * span, C + R)
    scale = 1.0 / math.sqrt(NOPE + R)
    cycle_size = lax.axis_size("ctx")
    me_index = lax.axis_index("ctx")
    local = jnp.arange(span, dtype=jnp.int32)
    own_block = pick_entries(block_order, jnp.reshape(me_index, (1,)))[0]
    query_pos = jnp.tile(own_block * span + local, heads)

    def update(carry, keys, key_pos):
        top_old, total_old, summed_old = carry
        score = jnp.dot(query_cat, keys, preferred_element_type=jnp.float32) * scale
        visible = key_pos[None, :] <= query_pos[:, None]
        score = jnp.where(visible, score, NEG)
        top_new = jnp.maximum(top_old, jnp.max(score, axis=1))
        expo = jnp.where(visible, jnp.exp(score - top_new[:, None]), 0.0)
        factor = jnp.exp(top_old - top_new)
        total_new = total_old * factor + jnp.sum(expo, axis=1)
        contrib = lax.dot_general(
            expo.astype(jnp.bfloat16),
            keys[:C],
            (((1,), (1,)), ((), ())),
            preferred_element_type=jnp.float32,
        )
        return (top_new, total_new, summed_old * factor[:, None] + contrib)

    def admit(carry, keys, key_pos):
        return update(carry, keys, key_pos)

    row_count = heads * span
    initial = (
        jnp.full((row_count,), NEG, jnp.float32),
        jnp.zeros((row_count,), jnp.float32),
        jnp.zeros((row_count, C), jnp.float32),
    )

    def turn(step, state):
        carry, keys = state
        source = jnp.mod(me_index - step, cycle_size)
        block = pick_entries(block_order, jnp.reshape(source, (1,)))[0]
        carry = admit(carry, keys, block * span + local)
        keys = from_behind(keys, "ctx", 1)
        return (carry, keys)

    carry, keys = lax.fori_loop(0, cycle_size - 1, turn, (initial, latents))
    source = jnp.mod(me_index + 1, cycle_size)
    block = pick_entries(block_order, jnp.reshape(source, (1,)))[0]
    carry = admit(carry, keys, block * span + local)
    top_final, total_final, summed_final = carry
    mixed = (summed_final / total_final[:, None]).astype(jnp.bfloat16).reshape(heads, span, C)
    head_out = (
        jnp.einsum("htc,hcv->thv", mixed, w_value, preferred_element_type=jnp.float32)
        .astype(jnp.bfloat16)
        .reshape(span, heads * V)
    )
    return lax.psum_scatter(
        lax.dot_general(
            w_out, head_out, (((0,), (1,)), ((), ())), preferred_element_type=jnp.float32
        ).astype(jnp.bfloat16),
        "head",
        scatter_dimension=0,
        tiled=True,
    )


def solution(mesh):
    return jax.shard_map(
        shards,
        mesh=mesh,
        in_specs=(
            P("ctx", "head"),
            P(None, "ctx"),
            P("head", None, None),
            P("head", None, None),
            P("head", None),
            P(),
        ),
        out_specs=P("head", "ctx"),
        check_vma=False,
    )
```

profile of v0, /device:TPU:1, one launch (start us, length us, event | category | flops | bytes accessed | tf_op | source)
XLA Modules:
  0.0 370.8 jit_solution(673682149324756484)
XLA Ops:
  13.3 3.4 pad_maximum_fusion
  16.7 292.5 %while.22 = (s32[]{:T(128)}, f32[2048]{0:T(1024)S(1)}, f32[2048]{0:T(1024)S(1)}, f32[2048,512]{1,0:T(8,128)}, bf16[576,128]{1,0:T(8,128)(2,1)S(1)}, /*index=5*/s...) while((s32[]{:T(128)}, f32[2048]{0:T(1024)S(1)}, ...), condition=%wide.region_5.6_spmd.clone, body=%wide.region_1.5_spmd.clone.sunk | while | flops 576727296 | bytes 48778240 | solution.py:80
  29.9 2.9 fusion.56
  39.2 2.9 fusion.56
  48.4 2.9 fusion.56
  58.0 2.9 fusion.56
  67.6 2.9 fusion.56
  76.9 2.9 fusion.56
  86.0 2.9 fusion.56
  95.6 2.9 fusion.56
  105.2 2.9 fusion.56
  114.5 2.9 fusion.56
  123.4 2.9 fusion.56
  133.0 2.9 fusion.56
  142.5 2.9 fusion.56
  151.8 2.9 fusion.56
  161.3 2.9 fusion.56
  170.9 2.9 fusion.56
  180.5 2.9 fusion.56
  189.8 2.9 fusion.56
  199.0 2.9 fusion.56
  208.6 2.9 fusion.56
  218.2 2.9 fusion.56
  227.4 2.9 fusion.56
  236.6 2.9 fusion.56
  246.2 2.9 fusion.56
  255.8 2.9 fusion.56
  265.1 2.9 fusion.56
  273.9 2.9 fusion.56
  293.1 2.9 fusion.56
  314.7 3.5 copy-done.4
  321.6 42.4 %reduce-scatter.4.cloned.1.call-done = bf16[896,128]{1,0:T(8,128)(2,1)} async-done(((bf16[3584,128]{1,0:T(8,128)(2,1)}), bf16[896,128]{1,0:T(8,128)(2,1)}) %reduce-scatter.4.cloned.1.call-update) | async-done | bytes 229392 | tf_op jit(solution)/shard_map/reduce_scatter | solution.py:91
  (500 shorter events, 202.0 us)
Async XLA Ops:
  6.5 357.5 %reduce-scatter.4.cloned.1.call-start = ((), (), s32[]{:S(2)}) async-start(), calls=%async_computation.1 | async-start | bytes 1146880 | tf_op jit(solution)/shard_map/reduce_scatter | solution.py:91
  16.7 10.8 %collective-permute-start = (bf16[576,128]{1,0:T(8,128)(2,1)S(1)}, bf16[576,128]{1,0:T(8,128)(2,1)S(1)}, u32[]{:S(2)}, u32[]{:S(2)}) collective-permute-start(bf16[576,128]{1,0:T(8,128)(2,1)S(1)} %copy.33), channel_id=1, source_target_pairs={{0,4},{4,8},{8,12},{12,16},{16,20},{20,24},{24,28},{28,32},{32,36}... | collective-permute-start | bytes 442376 | tf_op jit(solution)/shard_map/while/body/eval_jaxpr/ppermute | solution.py:20
  27.5 9.2 %collective-permute-start = (bf16[576,128]{1,0:T(8,128)(2,1)S(1)}, bf16[576,128]{1,0:T(8,128)(2,1)S(1)}, u32[]{:S(2)}, u32[]{:S(2)}) collective-permute-start(bf16[576,128]{1,0:T(8,128)(2,1)S(1)} %copy.33), channel_id=1, source_target_pairs={{0,4},{4,8},{8,12},{12,16},{16,20},{20,24},{24,28},{28,32},{32,36}... | collective-permute-start | bytes 442376 | tf_op jit(solution)/shard_map/while/body/eval_jaxpr/ppermute | solution.py:20
  36.7 9.3 %collective-permute-start = (bf16[576,128]{1,0:T(8,128)(2,1)S(1)}, bf16[576,128]{1,0:T(8,128)(2,1)S(1)}, u32[]{:S(2)}, u32[]{:S(2)}) collective-permute-start(bf16[576,128]{1,0:T(8,128)(2,1)S(1)} %copy.33), channel_id=1, source_target_pairs={{0,4},{4,8},{8,12},{12,16},{16,20},{20,24},{24,28},{28,32},{32,36}... | collective-permute-start | bytes 442376 | tf_op jit(solution)/shard_map/while/body/eval_jaxpr/ppermute | solution.py:20
  46.0 9.1 %collective-permute-start = (bf16[576,128]{1,0:T(8,128)(2,1)S(1)}, bf16[576,128]{1,0:T(8,128)(2,1)S(1)}, u32[]{:S(2)}, u32[]{:S(2)}) collective-permute-start(bf16[576,128]{1,0:T(8,128)(2,1)S(1)} %copy.33), channel_id=1, source_target_pairs={{0,4},{4,8},{8,12},{12,16},{16,20},{20,24},{24,28},{28,32},{32,36}... | collective-permute-start | bytes 442376 | tf_op jit(solution)/shard_map/while/body/eval_jaxpr/ppermute | solution.py:20
  55.2 9.6 %collective-permute-start = (bf16[576,128]{1,0:T(8,128)(2,1)S(1)}, bf16[576,128]{1,0:T(8,128)(2,1)S(1)}, u32[]{:S(2)}, u32[]{:S(2)}) collective-permute-start(bf16[576,128]{1,0:T(8,128)(2,1)S(1)} %copy.33), channel_id=1, source_target_pairs={{0,4},{4,8},{8,12},{12,16},{16,20},{20,24},{24,28},{28,32},{32,36}... | collective-permute-start | bytes 442376 | tf_op jit(solution)/shard_map/while/body/eval_jaxpr/ppermute | solution.py:20
  64.8 9.6 %collective-permute-start = (bf16[576,128]{1,0:T(8,128)(2,1)S(1)}, bf16[576,128]{1,0:T(8,128)(2,1)S(1)}, u32[]{:S(2)}, u32[]{:S(2)}) collective-permute-start(bf16[576,128]{1,0:T(8,128)(2,1)S(1)} %copy.33), channel_id=1, source_target_pairs={{0,4},{4,8},{8,12},{12,16},{16,20},{20,24},{24,28},{28,32},{32,36}... | collective-permute-start | bytes 442376 | tf_op jit(solution)/shard_map/while/body/eval_jaxpr/ppermute | solution.py:20
  74.4 9.3 %collective-permute-start = (bf16[576,128]{1,0:T(8,128)(2,1)S(1)}, bf16[576,128]{1,0:T(8,128)(2,1)S(1)}, u32[]{:S(2)}, u32[]{:S(2)}) collective-permute-start(bf16[576,128]{1,0:T(8,128)(2,1)S(1)} %copy.33), channel_id=1, source_target_pairs={{0,4},{4,8},{8,12},{12,16},{16,20},{20,24},{24,28},{28,32},{32,36}... | collective-permute-start | bytes 442376 | tf_op jit(solution)/shard_map/while/body/eval_jaxpr/ppermute | solution.py:20
  83.6 9.1 %collective-permute-start = (bf16[576,128]{1,0:T(8,128)(2,1)S(1)}, bf16[576,128]{1,0:T(8,128)(2,1)S(1)}, u32[]{:S(2)}, u32[]{:S(2)}) collective-permute-start(bf16[576,128]{1,0:T(8,128)(2,1)S(1)} %copy.33), channel_id=1, source_target_pairs={{0,4},{4,8},{8,12},{12,16},{16,20},{20,24},{24,28},{28,32},{32,36}... | collective-permute-start | bytes 442376 | tf_op jit(solution)/shard_map/while/body/eval_jaxpr/ppermute | solution.py:20
  92.8 9.6 %collective-permute-start = (bf16[576,128]{1,0:T(8,128)(2,1)S(1)}, bf16[576,128]{1,0:T(8,128)(2,1)S(1)}, u32[]{:S(2)}, u32[]{:S(2)}) collective-permute-start(bf16[576,128]{1,0:T(8,128)(2,1)S(1)} %copy.33), channel_id=1, source_target_pairs={{0,4},{4,8},{8,12},{12,16},{16,20},{20,24},{24,28},{28,32},{32,36}... | collective-permute-start | bytes 442376 | tf_op jit(solution)/shard_map/while/body/eval_jaxpr/ppermute | solution.py:20
  102.4 9.6 %collective-permute-start = (bf16[576,128]{1,0:T(8,128)(2,1)S(1)}, bf16[576,128]{1,0:T(8,128)(2,1)S(1)}, u32[]{:S(2)}, u32[]{:S(2)}) collective-permute-start(bf16[576,128]{1,0:T(8,128)(2,1)S(1)} %copy.33), channel_id=1, source_target_pairs={{0,4},{4,8},{8,12},{12,16},{16,20},{20,24},{24,28},{28,32},{32,36}... | collective-permute-start | bytes 442376 | tf_op jit(solution)/shard_map/while/body/eval_jaxpr/ppermute | solution.py:20
  112.0 9.3 %collective-permute-start = (bf16[576,128]{1,0:T(8,128)(2,1)S(1)}, bf16[576,128]{1,0:T(8,128)(2,1)S(1)}, u32[]{:S(2)}, u32[]{:S(2)}) collective-permute-start(bf16[576,128]{1,0:T(8,128)(2,1)S(1)} %copy.33), channel_id=1, source_target_pairs={{0,4},{4,8},{8,12},{12,16},{16,20},{20,24},{24,28},{28,32},{32,36}... | collective-permute-start | bytes 442376 | tf_op jit(solution)/shard_map/while/body/eval_jaxpr/ppermute | solution.py:20
  121.3 8.9 %collective-permute-start = (bf16[576,128]{1,0:T(8,128)(2,1)S(1)}, bf16[576,128]{1,0:T(8,128)(2,1)S(1)}, u32[]{:S(2)}, u32[]{:S(2)}) collective-permute-start(bf16[576,128]{1,0:T(8,128)(2,1)S(1)} %copy.33), channel_id=1, source_target_pairs={{0,4},{4,8},{8,12},{12,16},{16,20},{20,24},{24,28},{28,32},{32,36}... | collective-permute-start | bytes 442376 | tf_op jit(solution)/shard_map/while/body/eval_jaxpr/ppermute | solution.py:20
  130.2 9.6 %collective-permute-start = (bf16[576,128]{1,0:T(8,128)(2,1)S(1)}, bf16[576,128]{1,0:T(8,128)(2,1)S(1)}, u32[]{:S(2)}, u32[]{:S(2)}) collective-permute-start(bf16[576,128]{1,0:T(8,128)(2,1)S(1)} %copy.33), channel_id=1, source_target_pairs={{0,4},{4,8},{8,12},{12,16},{16,20},{20,24},{24,28},{28,32},{32,36}... | collective-permute-start | bytes 442376 | tf_op jit(solution)/shard_map/while/body/eval_jaxpr/ppermute | solution.py:20
  139.7 9.6 %collective-permute-start = (bf16[576,128]{1,0:T(8,128)(2,1)S(1)}, bf16[576,128]{1,0:T(8,128)(2,1)S(1)}, u32[]{:S(2)}, u32[]{:S(2)}) collective-permute-start(bf16[576,128]{1,0:T(8,128)(2,1)S(1)} %copy.33), channel_id=1, source_target_pairs={{0,4},{4,8},{8,12},{12,16},{16,20},{20,24},{24,28},{28,32},{32,36}... | collective-permute-start | bytes 442376 | tf_op jit(solution)/shard_map/while/body/eval_jaxpr/ppermute | solution.py:20
  149.3 9.3 %collective-permute-start = (bf16[576,128]{1,0:T(8,128)(2,1)S(1)}, bf16[576,128]{1,0:T(8,128)(2,1)S(1)}, u32[]{:S(2)}, u32[]{:S(2)}) collective-permute-start(bf16[576,128]{1,0:T(8,128)(2,1)S(1)} %copy.33), channel_id=1, source_target_pairs={{0,4},{4,8},{8,12},{12,16},{16,20},{20,24},{24,28},{28,32},{32,36}... | collective-permute-start | bytes 442376 | tf_op jit(solution)/shard_map/while/body/eval_jaxpr/ppermute | solution.py:20
  158.6 9.5 %collective-permute-start = (bf16[576,128]{1,0:T(8,128)(2,1)S(1)}, bf16[576,128]{1,0:T(8,128)(2,1)S(1)}, u32[]{:S(2)}, u32[]{:S(2)}) collective-permute-start(bf16[576,128]{1,0:T(8,128)(2,1)S(1)} %copy.33), channel_id=1, source_target_pairs={{0,4},{4,8},{8,12},{12,16},{16,20},{20,24},{24,28},{28,32},{32,36}... | collective-permute-start | bytes 442376 | tf_op jit(solution)/shard_map/while/body/eval_jaxpr/ppermute | solution.py:20
  168.1 9.6 %collective-permute-start = (bf16[576,128]{1,0:T(8,128)(2,1)S(1)}, bf16[576,128]{1,0:T(8,128)(2,1)S(1)}, u32[]{:S(2)}, u32[]{:S(2)}) collective-permute-start(bf16[576,128]{1,0:T(8,128)(2,1)S(1)} %copy.33), channel_id=1, source_target_pairs={{0,4},{4,8},{8,12},{12,16},{16,20},{20,24},{24,28},{28,32},{32,36}... | collective-permute-start | bytes 442376 | tf_op jit(solution)/shard_map/while/body/eval_jaxpr/ppermute | solution.py:20
  177.7 9.6 %collective-permute-start = (bf16[576,128]{1,0:T(8,128)(2,1)S(1)}, bf16[576,128]{1,0:T(8,128)(2,1)S(1)}, u32[]{:S(2)}, u32[]{:S(2)}) collective-permute-start(bf16[576,128]{1,0:T(8,128)(2,1)S(1)} %copy.33), channel_id=1, source_target_pairs={{0,4},{4,8},{8,12},{12,16},{16,20},{20,24},{24,28},{28,32},{32,36}... | collective-permute-start | bytes 442376 | tf_op jit(solution)/shard_map/while/body/eval_jaxpr/ppermute | solution.py:20
  187.3 9.3 %collective-permute-start = (bf16[576,128]{1,0:T(8,128)(2,1)S(1)}, bf16[576,128]{1,0:T(8,128)(2,1)S(1)}, u32[]{:S(2)}, u32[]{:S(2)}) collective-permute-start(bf16[576,128]{1,0:T(8,128)(2,1)S(1)} %copy.33), channel_id=1, source_target_pairs={{0,4},{4,8},{8,12},{12,16},{16,20},{20,24},{24,28},{28,32},{32,36}... | collective-permute-start | bytes 442376 | tf_op jit(solution)/shard_map/while/body/eval_jaxpr/ppermute | solution.py:20
  196.6 9.1 %collective-permute-start = (bf16[576,128]{1,0:T(8,128)(2,1)S(1)}, bf16[576,128]{1,0:T(8,128)(2,1)S(1)}, u32[]{:S(2)}, u32[]{:S(2)}) collective-permute-start(bf16[576,128]{1,0:T(8,128)(2,1)S(1)} %copy.33), channel_id=1, source_target_pairs={{0,4},{4,8},{8,12},{12,16},{16,20},{20,24},{24,28},{28,32},{32,36}... | collective-permute-start | bytes 442376 | tf_op jit(solution)/shard_map/while/body/eval_jaxpr/ppermute | solution.py:20
  205.8 9.6 %collective-permute-start = (bf16[576,128]{1,0:T(8,128)(2,1)S(1)}, bf16[576,128]{1,0:T(8,128)(2,1)S(1)}, u32[]{:S(2)}, u32[]{:S(2)}) collective-permute-start(bf16[576,128]{1,0:T(8,128)(2,1)S(1)} %copy.33), channel_id=1, source_target_pairs={{0,4},{4,8},{8,12},{12,16},{16,20},{20,24},{24,28},{28,32},{32,36}... | collective-permute-start | bytes 442376 | tf_op jit(solution)/shard_map/while/body/eval_jaxpr/ppermute | solution.py:20
  215.4 9.6 %collective-permute-start = (bf16[576,128]{1,0:T(8,128)(2,1)S(1)}, bf16[576,128]{1,0:T(8,128)(2,1)S(1)}, u32[]{:S(2)}, u32[]{:S(2)}) collective-permute-start(bf16[576,128]{1,0:T(8,128)(2,1)S(1)} %copy.33), channel_id=1, source_target_pairs={{0,4},{4,8},{8,12},{12,16},{16,20},{20,24},{24,28},{28,32},{32,36}... | collective-permute-start | bytes 442376 | tf_op jit(solution)/shard_map/while/body/eval_jaxpr/ppermute | solution.py:20
  224.9 9.3 %collective-permute-start = (bf16[576,128]{1,0:T(8,128)(2,1)S(1)}, bf16[576,128]{1,0:T(8,128)(2,1)S(1)}, u32[]{:S(2)}, u32[]{:S(2)}) collective-permute-start(bf16[576,128]{1,0:T(8,128)(2,1)S(1)} %copy.33), channel_id=1, source_target_pairs={{0,4},{4,8},{8,12},{12,16},{16,20},{20,24},{24,28},{28,32},{32,36}... | collective-permute-start | bytes 442376 | tf_op jit(solution)/shard_map/while/body/eval_jaxpr/ppermute | solution.py:20
  234.2 9.1 %collective-permute-start = (bf16[576,128]{1,0:T(8,128)(2,1)S(1)}, bf16[576,128]{1,0:T(8,128)(2,1)S(1)}, u32[]{:S(2)}, u32[]{:S(2)}) collective-permute-start(bf16[576,128]{1,0:T(8,128)(2,1)S(1)} %copy.33), channel_id=1, source_target_pairs={{0,4},{4,8},{8,12},{12,16},{16,20},{20,24},{24,28},{28,32},{32,36}... | collective-permute-start | bytes 442376 | tf_op jit(solution)/shard_map/while/body/eval_jaxpr/ppermute | solution.py:20
  243.4 9.6 %collective-permute-start = (bf16[576,128]{1,0:T(8,128)(2,1)S(1)}, bf16[576,128]{1,0:T(8,128)(2,1)S(1)}, u32[]{:S(2)}, u32[]{:S(2)}) collective-permute-start(bf16[576,128]{1,0:T(8,128)(2,1)S(1)} %copy.33), channel_id=1, source_target_pairs={{0,4},{4,8},{8,12},{12,16},{16,20},{20,24},{24,28},{28,32},{32,36}... | collective-permute-start | bytes 442376 | tf_op jit(solution)/shard_map/while/body/eval_jaxpr/ppermute | solution.py:20
  253.0 9.6 %collective-permute-start = (bf16[576,128]{1,0:T(8,128)(2,1)S(1)}, bf16[576,128]{1,0:T(8,128)(2,1)S(1)}, u32[]{:S(2)}, u32[]{:S(2)}) collective-permute-start(bf16[576,128]{1,0:T(8,128)(2,1)S(1)} %copy.33), channel_id=1, source_target_pairs={{0,4},{4,8},{8,12},{12,16},{16,20},{20,24},{24,28},{28,32},{32,36}... | collective-permute-start | bytes 442376 | tf_op jit(solution)/shard_map/while/body/eval_jaxpr/ppermute | solution.py:20
  262.6 9.3 %collective-permute-start = (bf16[576,128]{1,0:T(8,128)(2,1)S(1)}, bf16[576,128]{1,0:T(8,128)(2,1)S(1)}, u32[]{:S(2)}, u32[]{:S(2)}) collective-permute-start(bf16[576,128]{1,0:T(8,128)(2,1)S(1)} %copy.33), channel_id=1, source_target_pairs={{0,4},{4,8},{8,12},{12,16},{16,20},{20,24},{24,28},{28,32},{32,36}... | collective-permute-start | bytes 442376 | tf_op jit(solution)/shard_map/while/body/eval_jaxpr/ppermute | solution.py:20
  271.9 8.9 %collective-permute-start = (bf16[576,128]{1,0:T(8,128)(2,1)S(1)}, bf16[576,128]{1,0:T(8,128)(2,1)S(1)}, u32[]{:S(2)}, u32[]{:S(2)}) collective-permute-start(bf16[576,128]{1,0:T(8,128)(2,1)S(1)} %copy.33), channel_id=1, source_target_pairs={{0,4},{4,8},{8,12},{12,16},{16,20},{20,24},{24,28},{28,32},{32,36}... | collective-permute-start | bytes 442376 | tf_op jit(solution)/shard_map/while/body/eval_jaxpr/ppermute | solution.py:20
  280.8 9.9 %collective-permute-start = (bf16[576,128]{1,0:T(8,128)(2,1)S(1)}, bf16[576,128]{1,0:T(8,128)(2,1)S(1)}, u32[]{:S(2)}, u32[]{:S(2)}) collective-permute-start(bf16[576,128]{1,0:T(8,128)(2,1)S(1)} %copy.33), channel_id=1, source_target_pairs={{0,4},{4,8},{8,12},{12,16},{16,20},{20,24},{24,28},{28,32},{32,36}... | collective-permute-start | bytes 442376 | tf_op jit(solution)/shard_map/while/body/eval_jaxpr/ppermute | solution.py:20
  290.7 9.1 %collective-permute-start = (bf16[576,128]{1,0:T(8,128)(2,1)S(1)}, bf16[576,128]{1,0:T(8,128)(2,1)S(1)}, u32[]{:S(2)}, u32[]{:S(2)}) collective-permute-start(bf16[576,128]{1,0:T(8,128)(2,1)S(1)} %copy.33), channel_id=1, source_target_pairs={{0,4},{4,8},{8,12},{12,16},{16,20},{20,24},{24,28},{28,32},{32,36}... | collective-permute-start | bytes 442376 | tf_op jit(solution)/shard_map/while/body/eval_jaxpr/ppermute | solution.py:20
  299.9 9.3 %collective-permute-start = (bf16[576,128]{1,0:T(8,128)(2,1)S(1)}, bf16[576,128]{1,0:T(8,128)(2,1)S(1)}, u32[]{:S(2)}, u32[]{:S(2)}) collective-permute-start(bf16[576,128]{1,0:T(8,128)(2,1)S(1)} %copy.33), channel_id=1, source_target_pairs={{0,4},{4,8},{8,12},{12,16},{16,20},{20,24},{24,28},{28,32},{32,36}... | collective-permute-start | bytes 442376 | tf_op jit(solution)/shard_map/while/body/eval_jaxpr/ppermute | solution.py:20
  (68 other events, 182.4 us)
Sparse Core Ops, SparseCore 0:
  321.7 42.2 reduce-scatter.3
where the time goes:
time: 371 us
  matrix products  150 us (40%)
  local copies, waits for them, and re-layouts  66.9 us (18%)
  waiting for transfers between devices  43.4 us (12%)
  starting transfers between devices  36.6 us (10%)
  other arithmetic  35.8 us (10%)
  loops' own time  23.9 us (6%)
  between operations  14.7 us (4%)
    dot_general x32, matrix products, update(): score = jnp.dot(query_cat, keys, preferred_element_type=jnp.float32) * scale  92.5 us
    while x186, local copies, waits for them, and re-layouts  60 us
    dot_general x32, matrix products, update(): lax.dot_general(expo.astype(jnp.bfloat16), keys[:C], (((1,), (1,)), ((),...  52.1 us
    reduce_scatter x1, waiting for transfers between devices, shards(): lax.psum_scatter(lax.dot_general(w_out, head_out, (((0,), (1,)), ((), ())...  42.4 us
    ppermute x31, starting transfers between devices, from_behind(): return lax.ppermute(value, axis, pairs)  36.6 us
    another operation x1, loops' own time, shards(): carry, keys = lax.fori_loop(0, cycle_size - 1, turn, (initial, latents))  23.9 us
    reduce_sum x32, other arithmetic, pick_entries(): return jnp.sum(jnp.where(hits, table[None, :], 0), axis=1)  23.6 us
    reduce_sum x32, other arithmetic, update(): total_new = total_old * factor + jnp.sum(expo, axis=1)  8.07 us
  transfers between devices with their start and end apart: 32, of which 4 were waited for; matrix products, arithmetic and copies ran while one was open for 46% of the time, Pallas kernels for 0%

commit v1 on v0

v1 whole, which is shorter than its diff:
```python
import functools
import math

import jax
import jax.numpy as jnp
from jax import lax
from jax.experimental import pallas as pl
from jax.experimental.pallas import tpu as pltpu
from jax.sharding import PartitionSpec as P

NOPE = 128
R = 64
C = 512
V = 128
HEADS = 16
SPAN = 128
ROWS = HEADS * SPAN
BLOCKS = 32
KDIM = 640
TILE = 256
OWN_D = 896
NEG = -1e30
EXP_SCALE = math.log2(math.e) / math.sqrt(NOPE + R)
MESH = pl.DeviceIdType.MESH
F32 = jnp.float32
BF16 = jnp.bfloat16

CHUNKS = (
    ((0, 0),),
    ((1, 0), (3, 0), (0, 1), (0, 3)),
    ((2, 0), (1, 1), (1, 3), (3, 1)),
    ((3, 3), (2, 1), (2, 3), (0, 2)),
    ((1, 2), (2, 2), (3, 2)),
)


def slot_table():
    mine, other, bounds, at = {}, {}, [], 0
    for group in CHUNKS:
        first = at
        for table in (mine, other):
            for offset in group:
                table[offset] = at
                at += 1
        bounds.append((first, at))
    return mine, other, bounds


MINE, OTHER, BOUNDS = slot_table()
HALF_SEM = BLOCKS
N_RECV = BLOCKS + 1
N_SEND = 40


def kernel(
    q_hbm, lat_hbm, wk_hbm, wv_hbm, wo_hbm, order_ref, out_ref,
    q_ref, wk_ref, wv_ref, wo_ref, qc_ref, k_ref, kt_ref, mask_ref,
    m_ref, l_ref, acc_ref, s_ref, p_ref, a_ref, ho_ref,
    send_a, recv_a, send_b, recv_b, send_c, recv_c,
    load_sem, send_sem, recv_sem, rs_send, rs_recv,
):
    ci, hi = lax.axis_index("ctx"), lax.axis_index("head")
    z_lo, x, y = lax.div(ci, 16), lax.rem(lax.div(ci, 4), 4), lax.rem(ci, 4)
    z_hi, core = lax.div(hi, 2), lax.rem(hi, 2)
    sibling = (ci, z_hi * 2 + 1 - core)
    partner = (ci, (1 - z_hi) * 2 + core)
    z_near = ((1 - z_lo) * 16 + x * 4 + y, ((1 - core) * (1 - z_hi) + core * z_hi) * 2 + core)

    def place(along_core, z_low, du, dv):
        nx = lax.rem(x + (1 - along_core) * du + along_core * dv, 4)
        ny = lax.rem(y + (1 - along_core) * dv + along_core * du, 4)
        return z_low * 16 + nx * 4 + ny

    def at(du, dv):
        return (place(core, z_lo, du, dv), hi)

    around = [at(1, 0), at(3, 0), at(0, 1), at(0, 3)]

    def cols(slot):
        return pl.ds(slot * SPAN, SPAN) if isinstance(slot, int) else pl.ds(pl.multiple_of(slot * SPAN, SPAN), SPAN)

    def slab(slot, first=0, rows=C + R):
        return k_ref.at[pl.ds(first, rows), cols(slot)]

    sends = {}

    def send(src, dst, sem, device, rows=C + R):
        number = sends.setdefault(sem, (len(sends), rows))[0]
        pltpu.make_async_remote_copy(
            src_ref=src, dst_ref=dst, send_sem=send_sem.at[number], recv_sem=recv_sem.at[sem],
            device_id=device, device_id_type=MESH,
        ).start()

    def arrived(slot):
        pltpu.make_async_copy(slab(slot), slab(slot), recv_sem.at[slot]).wait()

    def arrived_half(first, sem):
        pltpu.make_async_copy(slab(0, first, 288), slab(0, first, 288), recv_sem.at[sem]).wait()

    def relay(offset):
        send(slab(MINE[offset]), slab(OTHER[offset]), OTHER[offset], sibling)

    def onward(src, dst, du, dv):
        send(slab(MINE[src]), slab(MINE[dst]), MINE[dst], at(du, dv))

    loads = [
        pltpu.make_async_copy(q_hbm, q_ref, load_sem.at[0]),
        pltpu.make_async_copy(wk_hbm, wk_ref, load_sem.at[1]),
        pltpu.make_async_copy(wv_hbm, wv_ref, load_sem.at[2]),
        pltpu.make_async_copy(wo_hbm, wo_ref, load_sem.at[3]),
    ]
    own_slot = core
    own_copy = pltpu.make_async_copy(lat_hbm, slab(own_slot), recv_sem.at[own_slot])
    own_copy.start()
    loads[0].start()
    loads[1].start()

    barrier = pltpu.get_barrier_semaphore()
    greeted = around + [sibling, partner, z_near]
    for device in greeted:
        pl.semaphore_signal(barrier, inc=1, device_id=device, device_id_type=MESH)
    pl.semaphore_wait(barrier, len(greeted))

    z_slot = 1 - core
    pltpu.make_async_remote_copy(
        src_ref=lat_hbm, dst_ref=slab(z_slot), send_sem=rs_send.at[3], recv_sem=recv_sem.at[z_slot],
        device_id=z_near, device_id_type=MESH,
    ).start()
    loads[2].start()
    loads[3].start()

    here = order_ref[ci]
    first_row = lax.broadcasted_iota(jnp.int32, (KDIM - C - R, SPAN), 0) == 0
    for group in CHUNKS:
        for table, along, z_low in (
            (MINE, core, (1 - core) * z_lo + core * (1 - z_lo)),
            (OTHER, 1 - core, core * z_lo + (1 - core) * (1 - z_lo)),
        ):
            for offset in group:
                block = order_ref[place(along, z_low, *offset)]
                bias = jnp.where(block <= here, 0.0, NEG)
                k_ref[C + R:, cols(table[offset])] = jnp.where(first_row, bias, 0.0).astype(BF16)
    token = lax.rem(lax.broadcasted_iota(jnp.int32, (TILE, 2 * SPAN), 0), SPAN)
    key = lax.broadcasted_iota(jnp.int32, (TILE, 2 * SPAN), 1)
    hidden = (lax.div(key, SPAN) == core) & (lax.rem(key, SPAN) > token)
    mask_ref[...] = jnp.where(hidden, NEG, 0.0)

    def spread():
        arrived(0)
        send(slab(0), slab(MINE[(3, 0)]), MINE[(3, 0)], around[0])
        send(slab(0), slab(MINE[(1, 0)]), MINE[(1, 0)], around[1])
        send(slab(0), slab(MINE[(0, 3)]), MINE[(0, 3)], around[2])
        send(slab(0), slab(MINE[(0, 1)]), MINE[(0, 1)], around[3])

    loads[0].wait()
    loads[1].wait()
    lane = lax.broadcasted_iota(jnp.int32, (SPAN, R), 1)
    one = jnp.where(lane == 0, 1.0, 0.0).astype(BF16)
    for h in range(HEADS):
        base = h * (NOPE + R)
        rows = slice(h * SPAN, (h + 1) * SPAN)
        qc_ref[rows, :C] = jnp.dot(
            q_ref[:, base:base + NOPE], wk_ref[h], preferred_element_type=F32
        ).astype(BF16)
        qc_ref[rows, C:] = jnp.concatenate([q_ref[:, base + NOPE:base + NOPE + R], one], axis=1)
    spread()
    arrived(1)

    tiles = ROWS // TILE

    def chunk(index, events):
        first, last = BOUNDS[index]
        width = (last - first) * SPAN
        keys = slice(first * SPAN, last * SPAN)
        begin = index == 0

        def rows_of(t):
            return pl.ds(t * TILE, TILE) if isinstance(t, int) else pl.ds(pl.multiple_of(t * TILE, TILE), TILE)

        def scores(t, b):
            s = jnp.dot(qc_ref[rows_of(t), :], k_ref[:, keys], preferred_element_type=F32)
            if begin:
                s = s + mask_ref[...]
            s_ref[b, :, :width] = s

        def soft(t, b):
            r = rows_of(t)
            s = s_ref[b, :, :width]
            top = jnp.max(s, axis=1, keepdims=True) * EXP_SCALE
            if begin:
                m_new = jnp.broadcast_to(top, (TILE, 128))
            else:
                m_old = m_ref[r, :]
                m_new = jnp.maximum(m_old, top)
                alpha = jnp.exp2(m_old - m_new)
                a_ref[b] = alpha
            wide = jnp.concatenate([m_new] * (width // 128), axis=1)
            e = jnp.exp2(s * EXP_SCALE - wide)
            part = e[:, :128]
            for i in range(1, width // 128):
                part = part + e[:, i * 128:(i + 1) * 128]
            l_ref[r, :] = part if begin else l_ref[r, :] * alpha + part
            m_ref[r, :] = m_new
            p_ref[b, :, :width] = e.astype(BF16)

        def values(t, b):
            r = rows_of(t)
            add = jnp.dot(p_ref[b, :, :width], kt_ref[:width, :], preferred_element_type=F32)
            if begin:
                acc_ref[r, :] = add
            else:
                acc_ref[r, :] = acc_ref[r, :] * jnp.concatenate([a_ref[b]] * 4, axis=1) + add

        kt_ref[:width, :] = k_ref[:C, keys].T
        scores(0, 0)
        scores(1, 1)
        soft(0, 0)

        def body(u, carry):
            for step, event in events.items():
                pl.when(u == step)(event)
            t = 2 * u + 2
            scores(t, 0)
            soft(t - 1, 1)
            values(t - 2, 0)
            scores(t + 1, 1)
            soft(t, 0)
            values(t - 1, 1)
            return carry

        lax.fori_loop(0, (tiles - 2) // 2, body, 0)
        soft(tiles - 1, 1)
        values(tiles - 2, 0)
        values(tiles - 1, 1)

    def others(index):
        for offset in CHUNKS[index]:
            arrived(OTHER[offset])

    chunk(0, {})

    arrived(MINE[(1, 0)])
    relay((1, 0))
    arrived(MINE[(3, 0)])
    relay((3, 0))
    send(slab(MINE[(3, 0)], 0, 288), slab(MINE[(2, 0)], 0, 288), MINE[(2, 0)], around[0], 288)
    send(slab(MINE[(1, 0)], 288, 288), slab(MINE[(2, 0)], 288, 288), HALF_SEM, around[1], 288)
    for du in (1, 3):
        onward((du, 0), (du, 3), 0, 1)
        onward((du, 0), (du, 1), 0, 3)
    arrived(MINE[(0, 1)])
    relay((0, 1))
    arrived(MINE[(0, 3)])
    relay((0, 3))
    onward((0, 3), (0, 2), 0, 1)
    others(1)

    def line_end():
        arrived_half(0, MINE[(2, 0)])
        arrived_half(288, HALF_SEM)
        relay((2, 0))
        onward((2, 0), (2, 3), 0, 1)
        onward((2, 0), (2, 1), 0, 3)

    def second():
        for offset in ((1, 1), (1, 3), (3, 1)):
            arrived(MINE[offset])
            relay(offset)
        onward((1, 3), (1, 2), 0, 1)
        onward((3, 1), (3, 2), 0, 3)

    def third():
        for offset in ((3, 3), (2, 1), (2, 3), (0, 2)):
            arrived(MINE[offset])
            relay(offset)
        onward((2, 1), (2, 2), 0, 3)

    def fourth():
        for offset in CHUNKS[4]:
            arrived(MINE[offset])
            relay(offset)

    chunk(1, {0: line_end, 2: second})
    others(2)
    chunk(2, {2: third})
    others(3)
    chunk(3, {1: fourth})
    others(4)
    chunk(4, {})

    loads[2].wait()
    for h in range(HEADS):
        rows = slice(h * SPAN, (h + 1) * SPAN)
        total = jnp.sum(l_ref[rows, :], axis=1, keepdims=True)
        mixed = (acc_ref[rows, :] / total).astype(BF16)
        ho_ref[:, h * V:(h + 1) * V] = jnp.dot(mixed, wv_ref[h], preferred_element_type=F32).astype(BF16)
    loads[3].wait()

    def project(zh, c):
        at_col = pl.multiple_of((zh * 2 + c) * OWN_D, 128)
        return jnp.dot(ho_ref[...], wo_ref[:, pl.ds(at_col, OWN_D)], preferred_element_type=F32)

    def rs(src, dst, n, device):
        copy = pltpu.make_async_remote_copy(
            src_ref=src, dst_ref=dst, send_sem=rs_send.at[n], recv_sem=rs_recv.at[n],
            device_id=device, device_id_type=MESH,
        )
        copy.start()
        return copy

    send_a[...] = project(1 - z_hi, 1 - core).astype(BF16)
    copy_a = rs(send_a, recv_a, 0, sibling)
    s_ref[0, :SPAN, :OWN_D] = project(1 - z_hi, core)
    copy_a.wait()
    send_b[...] = (s_ref[0, :SPAN, :OWN_D] + recv_a[...].astype(F32)).astype(BF16)
    copy_b = rs(send_b, recv_b, 1, partner)
    send_c[...] = project(z_hi, 1 - core).astype(BF16)
    copy_c = rs(send_c, recv_c, 2, sibling)
    s_ref[1, :SPAN, :OWN_D] = project(z_hi, core)
    copy_c.wait()
    s_ref[1, :SPAN, :OWN_D] = s_ref[1, :SPAN, :OWN_D] + recv_c[...].astype(F32)
    pltpu.make_async_copy(lat_hbm, lat_hbm, rs_send.at[3]).wait()
    for number, rows in sends.values():
        pltpu.make_async_copy(slab(0, 0, rows), slab(0, 0, rows), send_sem.at[number]).wait()
    copy_b.wait()
    out_ref[...] = (s_ref[1, :SPAN, :OWN_D] + recv_b[...].astype(F32)).T.astype(BF16)


def shards(queries, latents, w_key, w_value, w_out, block_order):
    any_spec = pl.BlockSpec(memory_space=pl.ANY)
    flops = 2 * ROWS * BLOCKS * SPAN * (KDIM + C)
    return pl.pallas_call(
        kernel,
        out_shape=jax.ShapeDtypeStruct((OWN_D, SPAN), BF16),
        in_specs=[any_spec] * 5 + [pl.BlockSpec(memory_space=pltpu.SMEM)],
        out_specs=pl.BlockSpec(memory_space=pltpu.VMEM),
        scratch_shapes=[
            pltpu.VMEM((SPAN, HEADS * (NOPE + R)), BF16),
            pltpu.VMEM((HEADS, NOPE, C), BF16),
            pltpu.VMEM((HEADS, C, V), BF16),
            pltpu.VMEM((HEADS * V, 4 * OWN_D), BF16),
            pltpu.VMEM((ROWS, KDIM), BF16),
            pltpu.VMEM((KDIM, BLOCKS * SPAN), BF16),
            pltpu.VMEM((1024, C), BF16),
            pltpu.VMEM((TILE, 2 * SPAN), F32),
            pltpu.VMEM((ROWS, 128), F32),
            pltpu.VMEM((ROWS, 128), F32),
            pltpu.VMEM((ROWS, C), F32),
            pltpu.VMEM((2, TILE, 1024), F32),
            pltpu.VMEM((2, TILE, 1024), BF16),
            pltpu.VMEM((2, TILE, 128), F32),
            pltpu.VMEM((SPAN, HEADS * V), BF16),
        ] + [pltpu.VMEM((SPAN, OWN_D), BF16)] * 6 + [
            pltpu.SemaphoreType.DMA((4,)),
            pltpu.SemaphoreType.DMA((N_SEND,)),
            pltpu.SemaphoreType.DMA((N_RECV,)),
            pltpu.SemaphoreType.DMA((4,)),
            pltpu.SemaphoreType.DMA((3,)),
        ],
        compiler_params=pltpu.CompilerParams(
            collective_id=0, has_side_effects=True, vmem_limit_bytes=58 * 2**20
        ),
        cost_estimate=pl.CostEstimate(flops=flops, bytes_accessed=20 * 2**20, transcendentals=ROWS * BLOCKS * SPAN),
        name="latent_attention",
    )(queries, latents, w_key, w_value, w_out, block_order)


def solution(mesh):
    return jax.shard_map(
        shards,
        mesh=mesh,
        in_specs=(
            P("ctx", "head"),
            P(None, "ctx"),
            P("head", None, None),
            P("head", None, None),
            P("head", None),
            P(),
        ),
        out_specs=P("head", "ctx"),
        check_vma=False,
    )
```

time: 371 us -> 59.3 us (0.16)
  matrix products: 150 us -> 0 us
  local copies, waits for them, and re-layouts: 66.9 us -> 1.64 us
  Pallas kernels: 0 us -> 57.5 us
  waiting for transfers between devices: 43.4 us -> 0 us
  starting transfers between devices: 36.6 us -> 0 us
  other arithmetic: 35.8 us -> 0 us
  loops' own time: 23.9 us -> 0 us
  between operations: 14.7 us -> 0.01 us
    dot_general x67 -> x0, matrix products: 150 us -> none  [the longest x32 92.5 us: update(): score = jnp.dot(query_cat, keys, preferred_element_type=jnp.float32) * scale]
    while x186 -> x0, local copies, waits for them, and re-layouts: 60 us -> none
    pallas_call x0 -> x1, Pallas kernels: none -> 57.5 us  [shards(): pl.pallas_call(kernel, out_shape=jax.ShapeDtypeStruct((OWN_D, SPAN), BF16...]
    reduce_scatter x1 -> x0, waiting for transfers between devices: 42.4 us -> none  [shards(): lax.psum_scatter(lax.dot_general(w_out, head_out, (((0,), (1,)), ((), ())...]
    ppermute x31 -> x0, starting transfers between devices: 36.6 us -> none  [from_behind(): return lax.ppermute(value, axis, pairs)]
    reduce_sum x64 -> x0, other arithmetic: 31.6 us -> none  [the longest x32 23.6 us: pick_entries(): return jnp.sum(jnp.where(hits, table[None, :], 0), axis=1)]
    another operation x1 -> x0, loops' own time: 23.9 us -> none  [shards(): carry, keys = lax.fori_loop(0, cycle_size - 1, turn, (initial, latents))]
    unnamed x15 -> x1, local copies, waits for them, and re-layouts: 6.8 us -> 1.64 us
  transfers between devices with their start and end apart: 32 -> 0, of which waited for: 4 -> 0; matrix products, arithmetic and copies ran while one was open for 46% -> 0% of each run, Pallas kernels for 0% -> 0%
where the time goes in v1:
time: 59.3 us; the launch traced here: 59.2 us
  Pallas kernels  57.5 us (97%)
  local copies, waits for them, and re-layouts  1.64 us (3%)
    pallas_call x1, Pallas kernels, shards(): pl.pallas_call(kernel, out_shape=jax.ShapeDtypeStruct((OWN_D, SPAN), BF16...  57.5 us
    unnamed x1, local copies, waits for them, and re-layouts  1.64 us

profile of v1, /device:TPU:1, one launch (start us, length us, event | category | flops | bytes accessed | tf_op | source)
XLA Modules:
  0.0 59.2 jit_solution(982921421221065033)
XLA Ops:
  0.0 57.5 %latent_attention.1 = bf16[896,128]{1,0:T(8,128)(2,1)} custom-call(bf16[128,3072]{1,0:T(8,128)(2,1)} %q_hbm.1, bf16[576,128]{1,0:T(8,128)(2,1)} %lat_hbm.1, bf16[16,128,512]{2,1,0:T(8,128)(2,1)} %wk_hbm.1, bf16[16,512,128]{2,1,0:T(8,128)(2,1)} %wv_hbm.1, bf16[2048,3584]{1,0:T(8,128)(2,1)} %wo_hbm.1, s32[32]{0:T(128)} %order_ref.1), custom_call_target="tpu_custom_call" | custom-call | flops 19327352832 | bytes 20971520 | tf_op jit(solution)/shard_map/latent_attention/pallas_call | solution.py:332
  57.5 1.6 %copy.8 = bf16[896,128]{1,0:T(8,128)(2,1)} copy(bf16[896,128]{1,0:T(8,128)(2,1)} %latent_attention.1) | data formatting | bytes 458752

commit v2 on v1

v2 whole, which is shorter than its diff:
```python
import functools
import math

import jax
import jax.numpy as jnp
from jax import lax
from jax.experimental import pallas as pl
from jax.experimental.pallas import tpu as pltpu
from jax.sharding import PartitionSpec as P

NOPE = 128
R = 64
C = 512
V = 128
HEADS = 16
SPAN = 128
ROWS = HEADS * SPAN
BLOCKS = 32
KDIM = 640
TILE = 512
OWN_D = 896
NEG = -1e30
EXP_SCALE = math.log2(math.e) / math.sqrt(NOPE + R)
MESH = pl.DeviceIdType.MESH
F32 = jnp.float32
BF16 = jnp.bfloat16

FETCHED = ("10", "30", "20", "13", "31", "21", "23")
CHUNKS = (
    ("OWN",),
    ("Z00", "M10", "M30"),
    ("O10", "O30", "M20", "O20"),
    ("M13", "M31", "MZ10", "MZ30"),
    ("O13", "O31", "OZ10", "OZ30", "M21", "M23", "O21", "O23"),
    ("P22", "MZ20", "OZ20", "MZ13", "MZ31", "OZ13", "OZ31", "MZ21"),
    ("MZ23", "OZ21", "OZ23", "Z22"),
)
ORDER = [name for group in CHUNKS for name in group]
SLOT = {name: number for number, name in enumerate(ORDER)}
P22_HALF, Z22_HALF = BLOCKS, BLOCKS + 1
N_RECV = BLOCKS + 2
N_SEND = 48
HALF = (C + R) // 2


def kernel(
    q_hbm, lat_hbm, wk_hbm, wv_hbm, wo_hbm, order_ref, out_ref,
    q_ref, wk_ref, wv_ref, wo_ref, qc_ref, k_ref, kt_ref, mask_ref,
    m_ref, l_ref, acc_ref, s_ref, p_ref, a_ref, ho_ref,
    send_a, recv_a, send_b, recv_b, send_c, recv_c,
    load_sem, send_sem, recv_sem, rs_send, rs_recv,
):
    ci, hi = lax.axis_index("ctx"), lax.axis_index("head")
    z_lo, x, y = lax.div(ci, 16), lax.rem(lax.div(ci, 4), 4), lax.rem(ci, 4)
    z_hi, core = lax.div(hi, 2), lax.rem(hi, 2)
    sibling = (ci, z_hi * 2 + 1 - core)
    partner = (ci, (1 - z_hi) * 2 + core)
    z_near = ((1 - z_lo) * 16 + x * 4 + y, ((1 - core) * (1 - z_hi) + core * z_hi) * 2 + core)

    def place(along_core, z_low, du, dw):
        nx = lax.rem(x + (1 - along_core) * du + along_core * dw, 4)
        ny = lax.rem(y + (1 - along_core) * (4 - dw) + along_core * du, 4)
        return z_low * 16 + nx * 4 + ny

    def at(du, dw):
        return (place(core, z_lo, du, dw), hi)

    def source(name):
        if name == "OWN":
            return ci
        z_low = 1 - z_lo if "Z" in name else z_lo
        along = 1 - core if "O" in name else core
        return place(along, z_low, int(name[-2]), int(name[-1]))

    def cols(slot):
        return pl.ds(slot * SPAN, SPAN)

    def slab(name, first=0, rows=C + R):
        return k_ref.at[pl.ds(first, rows), cols(SLOT[name])]

    half_at = pl.multiple_of(core * HALF, 32)

    def half(name):
        return slab(name, half_at, HALF)

    sends = {}

    def send(src, dst, key, sem, device, rows=C + R):
        number = sends.setdefault(key, (len(sends), rows))[0]
        pltpu.make_async_remote_copy(
            src_ref=src, dst_ref=dst, send_sem=send_sem.at[number], recv_sem=recv_sem.at[sem],
            device_id=device, device_id_type=MESH,
        ).start()

    def arrived(*names):
        for name in names:
            pltpu.make_async_copy(slab(name), slab(name), recv_sem.at[SLOT[name]]).wait()

    def arrived_half(sem):
        pltpu.make_async_copy(half("OWN"), half("OWN"), recv_sem.at[sem]).wait()

    def relay(*names):
        for name in names:
            there = name.replace("M", "O")
            send(slab(name), slab(there), there, SLOT[there], sibling)

    def along_z(*names):
        for name in names:
            there = "MZ" + name[1:]
            send(slab(name), slab(there), there, SLOT[there], z_near)

    def onward(name, there, device):
        send(slab(name), slab(there), there, SLOT[there], device)

    barrier = pltpu.get_barrier_semaphore()
    greeted = [
        at(2, 0), at(0, 2), at(1, 0), at(3, 0), at(0, 1), at(0, 3), z_near, partner, sibling,
    ]
    for device in greeted:
        pl.semaphore_signal(barrier, inc=1, device_id=device, device_id_type=MESH)

    own_copy = pltpu.make_async_copy(lat_hbm, slab("OWN"), load_sem.at[4])
    loads = [
        pltpu.make_async_copy(q_hbm, q_ref, load_sem.at[0]),
        pltpu.make_async_copy(wk_hbm, wk_ref, load_sem.at[1]),
        pltpu.make_async_copy(wv_hbm, wv_ref, load_sem.at[2]),
        pltpu.make_async_copy(wo_hbm, wo_ref, load_sem.at[3]),
    ]
    own_copy.start()
    for load in loads:
        load.start()

    here = order_ref[ci]
    first_row = lax.broadcasted_iota(jnp.int32, (KDIM - C - R, SPAN), 0) == 0
    for name in ORDER:
        bias = jnp.where(order_ref[source(name)] <= here, 0.0, NEG)
        k_ref[C + R:, cols(SLOT[name])] = jnp.where(first_row, bias, 0.0).astype(BF16)
    token = lax.rem(lax.broadcasted_iota(jnp.int32, (TILE, SPAN), 0), SPAN)
    key = lax.broadcasted_iota(jnp.int32, (TILE, SPAN), 1)
    mask_ref[...] = jnp.where(key > token, NEG, 0.0)

    loads[0].wait()
    loads[1].wait()
    lane = lax.broadcasted_iota(jnp.int32, (SPAN, R), 1)
    one = jnp.where(lane == 0, 1.0, 0.0).astype(BF16)
    for h in range(HEADS):
        base = h * (NOPE + R)
        rows = slice(h * SPAN, (h + 1) * SPAN)
        qc_ref[rows, :C] = jnp.dot(
            q_ref[:, base:base + NOPE], wk_ref[h], preferred_element_type=F32
        ).astype(BF16)
        qc_ref[rows, C:] = jnp.concatenate([q_ref[:, base + NOPE:base + NOPE + R], one], axis=1)
    own_copy.wait()

    tiles = ROWS // TILE

    def chunk(index, events=None):
        events = events or {}
        first = SLOT[CHUNKS[index][0]]
        last = first + len(CHUNKS[index])
        width = (last - first) * SPAN
        keys = slice(first * SPAN, last * SPAN)
        begin = index == 0

        def rows_of(t):
            return pl.ds(t * TILE, TILE) if isinstance(t, int) else pl.ds(pl.multiple_of(t * TILE, TILE), TILE)

        def scores(t, b):
            s = jnp.dot(qc_ref[rows_of(t), :], k_ref[:, keys], preferred_element_type=F32)
            if begin:
                s = s + mask_ref[...]
            s_ref[b, :, :width] = s

        def soft(t, b):
            r = rows_of(t)
            s = s_ref[b, :, :width]
            top = jnp.max(s, axis=1, keepdims=True) * EXP_SCALE
            if begin:
                m_new = jnp.broadcast_to(top, (TILE, 128))
            else:
                m_old = m_ref[r, :]
                m_new = jnp.maximum(m_old, top)
                alpha = jnp.exp2(m_old - m_new)
                a_ref[b] = alpha
            wide = jnp.concatenate([m_new] * (width // 128), axis=1)
            e = jnp.exp2(s * EXP_SCALE - wide)
            part = e[:, :128]
            for i in range(1, width // 128):
                part = part + e[:, i * 128:(i + 1) * 128]
            l_ref[r, :] = part if begin else l_ref[r, :] * alpha + part
            m_ref[r, :] = m_new
            p_ref[b, :, :width] = e.astype(BF16)

        def values(t, b):
            r = rows_of(t)
            add = jnp.dot(p_ref[b, :, :width], kt_ref[:width, :], preferred_element_type=F32)
            if begin:
                acc_ref[r, :] = add
            else:
                acc_ref[r, :] = acc_ref[r, :] * jnp.concatenate([a_ref[b]] * 4, axis=1) + add

        kt_ref[:width, :] = k_ref[:C, keys].T
        for step in range(tiles + 2):
            if step in events:
                events[step]()
            if step < tiles:
                scores(step, step % 2)
            if 0 <= step - 1 < tiles:
                soft(step - 1, (step - 1) % 2)
            if 0 <= step - 2 < tiles:
                values(step - 2, step % 2)

    chunk(0)
    pl.semaphore_wait(barrier, len(greeted))
    onward("OWN", "M30", at(1, 0))
    onward("OWN", "M10", at(3, 0))
    onward("OWN", "Z00", z_near)
    onward("OWN", "M20", at(2, 0))

    arrived("M10", "M30")
    relay("M10", "M30")
    onward("M10", "M13", at(0, 1))
    onward("M30", "M31", at(0, 3))
    along_z("M10", "M30")
    arrived("Z00")
    chunk(1)

    arrived("M20")
    relay("M20")
    onward("M20", "M23", at(0, 1))
    onward("M20", "M21", at(0, 3))
    send(half("M20"), half("P22"), "P22", SLOT["P22"], at(0, 2), HALF)
    along_z("M20")
    arrived("O10", "O30", "O20")
    chunk(2)

    arrived("M13", "M31")
    relay("M13", "M31")
    along_z("M13", "M31")
    arrived("MZ10", "MZ30")
    relay("MZ10", "MZ30")

    def third():
        arrived("M21", "M23")
        relay("M21", "M23")
        along_z("M21", "M23")
        arrived_half(SLOT["P22"])
        send(half("P22"), half("P22"), "P22r", P22_HALF, sibling, HALF)
        send(half("P22"), half("Z22"), "Z22", SLOT["Z22"], z_near, HALF)
        arrived("MZ20")
        relay("MZ20")

    chunk(3, {3: third})
    arrived("O13", "O31", "OZ10", "OZ30", "O21", "O23")

    def fourth():
        arrived("MZ13", "MZ31")
        relay("MZ13", "MZ31")

    def fifth():
        arrived("MZ21", "MZ23")
        relay("MZ21", "MZ23")
        arrived_half(SLOT["Z22"])
        send(half("Z22"), half("Z22"), "Z22r", Z22_HALF, sibling, HALF)

    chunk(4, {2: fourth, 4: fifth})
    arrived_half(P22_HALF)
    arrived("OZ20", "OZ13", "OZ31")
    chunk(5)
    arrived_half(Z22_HALF)
    arrived("OZ21", "OZ23")
    chunk(6)

    loads[2].wait()
    for h in range(HEADS):
        rows = slice(h * SPAN, (h + 1) * SPAN)
        total = jnp.sum(l_ref[rows, :], axis=1, keepdims=True)
        mixed = (acc_ref[rows, :] / total).astype(BF16)
        ho_ref[:, h * V:(h + 1) * V] = jnp.dot(mixed, wv_ref[h], preferred_element_type=F32).astype(BF16)
    loads[3].wait()

    pieces = ((0, 512), (512, 384))

    def project(zh, c, piece):
        at_col = pl.multiple_of((zh * 2 + c) * OWN_D + piece[0], 128)
        return jnp.dot(ho_ref[...], wo_ref[:, pl.ds(at_col, piece[1])], preferred_element_type=F32)

    def window(ref, piece):
        return ref.at[:, pl.ds(*piece)]

    def rs(src, dst, n, device):
        copy = pltpu.make_async_remote_copy(
            src_ref=src, dst_ref=dst, send_sem=rs_send.at[n], recv_sem=rs_recv.at[n],
            device_id=device, device_id_type=MESH,
        )
        copy.start()
        return copy

    copies_a, copies_b, copies_c = [], [], []
    for n, piece in enumerate(pieces):
        window(send_a, piece)[...] = project(1 - z_hi, 1 - core, piece).astype(BF16)
        copies_a.append(rs(window(send_a, piece), window(recv_a, piece), n, sibling))
    far = s_ref.at[0, pl.ds(0, SPAN)]
    near = s_ref.at[1, pl.ds(0, SPAN)]
    for piece in pieces:
        window(far, piece)[...] = project(1 - z_hi, core, piece)
    for n, piece in enumerate(pieces):
        window(send_c, piece)[...] = project(z_hi, 1 - core, piece).astype(BF16)
        copies_a[n].wait()
        window(send_b, piece)[...] = (window(far, piece)[...] + window(recv_a, piece)[...].astype(F32)).astype(BF16)
        copies_b.append(rs(window(send_b, piece), window(recv_b, piece), 2 + n, partner))
        copies_c.append(rs(window(send_c, piece), window(recv_c, piece), 4 + n, sibling))
    for piece in pieces:
        window(near, piece)[...] = project(z_hi, core, piece)
    for n, piece in enumerate(pieces):
        copies_c[n].wait()
        window(near, piece)[...] = window(near, piece)[...] + window(recv_c, piece)[...].astype(F32)
    for number, rows in sends.values():
        pltpu.make_async_copy(slab("OWN", 0, rows), slab("OWN", 0, rows), send_sem.at[number]).wait()
    for n, piece in enumerate(pieces):
        copies_b[n].wait()
        out_ref[pl.ds(*piece), :] = (window(near, piece)[...] + window(recv_b, piece)[...].astype(F32)).T.astype(BF16)


def shards(queries, latents, w_key, w_value, w_out, block_order):
    any_spec = pl.BlockSpec(memory_space=pl.ANY)
    flops = 2 * ROWS * BLOCKS * SPAN * (KDIM + C)
    return pl.pallas_call(
        kernel,
        out_shape=jax.ShapeDtypeStruct((OWN_D, SPAN), BF16),
        in_specs=[any_spec] * 5 + [pl.BlockSpec(memory_space=pltpu.SMEM)],
        out_specs=pl.BlockSpec(memory_space=pltpu.VMEM),
        scratch_shapes=[
            pltpu.VMEM((SPAN, HEADS * (NOPE + R)), BF16),
            pltpu.VMEM((HEADS, NOPE, C), BF16),
            pltpu.VMEM((HEADS, C, V), BF16),
            pltpu.VMEM((HEADS * V, 4 * OWN_D), BF16),
            pltpu.VMEM((ROWS, KDIM), BF16),
            pltpu.VMEM((KDIM, BLOCKS * SPAN), BF16),
            pltpu.VMEM((1024, C), BF16),
            pltpu.VMEM((TILE, SPAN), F32),
            pltpu.VMEM((ROWS, 128), F32),
            pltpu.VMEM((ROWS, 128), F32),
            pltpu.VMEM((ROWS, C), F32),
            pltpu.VMEM((2, TILE, 1024), F32),
            pltpu.VMEM((2, TILE, 1024), BF16),
            pltpu.VMEM((2, TILE, 128), F32),
            pltpu.VMEM((SPAN, HEADS * V), BF16),
        ] + [pltpu.VMEM((SPAN, OWN_D), BF16)] * 6 + [
            pltpu.SemaphoreType.DMA((5,)),
            pltpu.SemaphoreType.DMA((N_SEND,)),
            pltpu.SemaphoreType.DMA((N_RECV,)),
            pltpu.SemaphoreType.DMA((6,)),
            pltpu.SemaphoreType.DMA((6,)),
        ],
        compiler_params=pltpu.CompilerParams(
            collective_id=0, has_side_effects=True, vmem_limit_bytes=58 * 2**20
        ),
        cost_estimate=pl.CostEstimate(flops=flops, bytes_accessed=20 * 2**20, transcendentals=ROWS * BLOCKS * SPAN),
        name="latent_attention",
    )(queries, latents, w_key, w_value, w_out, block_order)


def solution(mesh):
    return jax.shard_map(
        shards,
        mesh=mesh,
        in_specs=(
            P("ctx", "head"),
            P(None, "ctx"),
            P("head", None, None),
            P("head", None, None),
            P("head", None),
            P(),
        ),
        out_specs=P("head", "ctx"),
        check_vma=False,
    )
```

time: 59.3 us -> 55 us (0.927)
  Pallas kernels: 57.5 us -> 53.2 us
    pallas_call x1, Pallas kernels: 57.5 us -> 53.2 us  [shards(): pl.pallas_call(kernel, out_shape=jax.ShapeDtypeStruct((OWN_D, SPAN), BF16...]
where the time goes in v2:
time: 55 us; the launch traced here: 54.9 us
  Pallas kernels  53.2 us (97%)
  local copies, waits for them, and re-layouts  1.64 us (3%)
    pallas_call x1, Pallas kernels, shards(): pl.pallas_call(kernel, out_shape=jax.ShapeDtypeStruct((OWN_D, SPAN), BF16...  53.2 us
    unnamed x1, local copies, waits for them, and re-layouts  1.64 us

profile of v2, /device:TPU:1, one launch (start us, length us, event | category | flops | bytes accessed | tf_op | source)
XLA Modules:
  0.0 54.9 jit_solution(1970688315985640745)
XLA Ops:
  0.0 53.2 %latent_attention.1 = bf16[896,128]{1,0:T(8,128)(2,1)} custom-call(bf16[128,3072]{1,0:T(8,128)(2,1)} %q_hbm.1, bf16[576,128]{1,0:T(8,128)(2,1)} %lat_hbm.1, bf16[16,128,512]{2,1,0:T(8,128)(2,1)} %wk_hbm.1, bf16[16,512,128]{2,1,0:T(8,128)(2,1)} %wv_hbm.1, bf16[2048,3584]{1,0:T(8,128)(2,1)} %wo_hbm.1, s32[32]{0:T(128)} %order_ref.1), custom_call_target="tpu_custom_call" | custom-call | flops 19327352832 | bytes 20971520 | tf_op jit(solution)/shard_map/latent_attention/pallas_call | solution.py:328
  53.3 1.6 %copy.8 = bf16[896,128]{1,0:T(8,128)(2,1)} copy(bf16[896,128]{1,0:T(8,128)(2,1)} %latent_attention.1) | data formatting | bytes 458752

commit v3 on v2

--- a/solution.py
+++ b/solution.py
@@ -25,7 +25,6 @@
 F32 = jnp.float32
 BF16 = jnp.bfloat16
 
-FETCHED = ("10", "30", "20", "13", "31", "21", "23")
 CHUNKS = (
     ("OWN",),
     ("Z00", "M10", "M30"),
@@ -35,6 +34,7 @@
     ("P22", "MZ20", "OZ20", "MZ13", "MZ31", "OZ13", "OZ31", "MZ21"),
     ("MZ23", "OZ21", "OZ23", "Z22"),
 )
+WIDEST = max(len(group) for group in CHUNKS) * 128
 ORDER = [name for group in CHUNKS for name in group]
 SLOT = {name: number for number, name in enumerate(ORDER)}
 P22_HALF, Z22_HALF = BLOCKS, BLOCKS + 1
@@ -65,6 +65,9 @@
     def at(du, dw):
         return (place(core, z_lo, du, dw), hi)
 
+    u_up, u_down, u_far = at(1, 0), at(3, 0), at(2, 0)
+    w_up, w_down, w_far = at(0, 1), at(0, 3), at(0, 2)
+
     def source(name):
         if name == "OWN":
             return ci
@@ -72,11 +75,11 @@
         along = 1 - core if "O" in name else core
         return place(along, z_low, int(name[-2]), int(name[-1]))
 
-    def cols(slot):
-        return pl.ds(slot * SPAN, SPAN)
-
-    def slab(name, first=0, rows=C + R):
-        return k_ref.at[pl.ds(first, rows), cols(SLOT[name])]
+    def cols(slot, count=1):
+        return pl.ds(slot * SPAN, count * SPAN)
+
+    def slab(name, first=0, rows=C + R, count=1):
+        return k_ref.at[pl.ds(first, rows), cols(SLOT[name], count)]
 
     half_at = pl.multiple_of(core * HALF, 32)
 
@@ -85,8 +88,8 @@
 
     sends = {}
 
-    def send(src, dst, key, sem, device, rows=C + R):
-        number = sends.setdefault(key, (len(sends), rows))[0]
+    def send(src, dst, key, sem, device, rows=C + R, count=1):
+        number = sends.setdefault(key, (len(sends), rows, count))[0]
         pltpu.make_async_remote_copy(
             src_ref=src, dst_ref=dst, send_sem=send_sem.at[number], recv_sem=recv_sem.at[sem],
             device_id=device, device_id_type=MESH,
@@ -96,26 +99,25 @@
         for name in names:
             pltpu.make_async_copy(slab(name), slab(name), recv_sem.at[SLOT[name]]).wait()
 
+    def arrived_pair(*names):
+        for name in names:
+            pair = slab(name, count=2)
+            pltpu.make_async_copy(pair, pair, recv_sem.at[SLOT[name]]).wait()
+
     def arrived_half(sem):
         pltpu.make_async_copy(half("OWN"), half("OWN"), recv_sem.at[sem]).wait()
 
-    def relay(*names):
-        for name in names:
-            there = name.replace("M", "O")
-            send(slab(name), slab(there), there, SLOT[there], sibling)
-
-    def along_z(*names):
-        for name in names:
-            there = "MZ" + name[1:]
-            send(slab(name), slab(there), there, SLOT[there], z_near)
-
-    def onward(name, there, device):
-        send(slab(name), slab(there), there, SLOT[there], device)
+    def onward(name, there, device, count=1):
+        send(slab(name, count=count), slab(there, count=count), there, SLOT[there], device, count=count)
+
+    def relay(name, count=1):
+        onward(name, name.replace("M", "O"), sibling, count)
+
+    def along_z(name, count=1):
+        onward(name, "MZ" + name[1:], z_near, count)
 
     barrier = pltpu.get_barrier_semaphore()
-    greeted = [
-        at(2, 0), at(0, 2), at(1, 0), at(3, 0), at(0, 1), at(0, 3), z_near, partner, sibling,
-    ]
+    greeted = [u_far, w_far, u_up, u_down, w_up, w_down, z_near, partner, sibling]
     for device in greeted:
         pl.semaphore_signal(barrier, inc=1, device_id=device, device_id_type=MESH)
 
@@ -138,6 +140,13 @@
     token = lax.rem(lax.broadcasted_iota(jnp.int32, (TILE, SPAN), 0), SPAN)
     key = lax.broadcasted_iota(jnp.int32, (TILE, SPAN), 1)
     mask_ref[...] = jnp.where(key > token, NEG, 0.0)
+
+    own_copy.wait()
+    pl.semaphore_wait(barrier, len(greeted))
+    onward("OWN", "M30", u_up)
+    onward("OWN", "M10", u_down)
+    onward("OWN", "Z00", z_near)
+    onward("OWN", "M20", u_far)
 
     loads[0].wait()
     loads[1].wait()
@@ -150,11 +159,10 @@
             q_ref[:, base:base + NOPE], wk_ref[h], preferred_element_type=F32
         ).astype(BF16)
         qc_ref[rows, C:] = jnp.concatenate([q_ref[:, base + NOPE:base + NOPE + R], one], axis=1)
-    own_copy.wait()
 
     tiles = ROWS // TILE
 
-    def chunk(index, events=None):
+    def chunk(index, events=None, after=None):
         events = events or {}
         first = SLOT[CHUNKS[index][0]]
         last = first + len(CHUNKS[index])
@@ -209,77 +217,85 @@
                 soft(step - 1, (step - 1) % 2)
             if 0 <= step - 2 < tiles:
                 values(step - 2, step % 2)
+                if after is not None:
+                    after(step - 2)
 
     chunk(0)
-    pl.semaphore_wait(barrier, len(greeted))
-    onward("OWN", "M30", at(1, 0))
-    onward("OWN", "M10", at(3, 0))
-    onward("OWN", "Z00", z_near)
-    onward("OWN", "M20", at(2, 0))
-
     arrived("M10", "M30")
-    relay("M10", "M30")
-    onward("M10", "M13", at(0, 1))
-    onward("M30", "M31", at(0, 3))
-    along_z("M10", "M30")
+    onward("M10", "M13", w_up)
+    onward("M30", "M31", w_down)
+    along_z("M10", 2)
+    relay("M10", 2)
     arrived("Z00")
-    chunk(1)
-
-    arrived("M20")
-    relay("M20")
-    onward("M20", "M23", at(0, 1))
-    onward("M20", "M21", at(0, 3))
-    send(half("M20"), half("P22"), "P22", SLOT["P22"], at(0, 2), HALF)
-    along_z("M20")
-    arrived("O10", "O30", "O20")
-    chunk(2)
-
-    arrived("M13", "M31")
-    relay("M13", "M31")
-    along_z("M13", "M31")
-    arrived("MZ10", "MZ30")
-    relay("MZ10", "MZ30")
-
-    def third():
+
+    def two_away():
+        arrived("M20")
+        relay("M20")
+        onward("M20", "M23", w_up)
+        onward("M20", "M21", w_down)
+        send(half("M20"), half("P22"), "P22", SLOT["P22"], w_far, HALF)
+        along_z("M20")
+
+    chunk(1, {2: two_away})
+    arrived_pair("O10")
+    arrived("O20")
+
+    def diagonals():
+        arrived("M13", "M31")
+        relay("M13", 2)
+        along_z("M13", 2)
+
+    chunk(2, {4: diagonals})
+    arrived_pair("MZ10")
+    relay("MZ10", 2)
+
+    def corners():
         arrived("M21", "M23")
-        relay("M21", "M23")
-        along_z("M21", "M23")
+        relay("M21", 2)
+        along_z("M21", 2)
         arrived_half(SLOT["P22"])
         send(half("P22"), half("P22"), "P22r", P22_HALF, sibling, HALF)
         send(half("P22"), half("Z22"), "Z22", SLOT["Z22"], z_near, HALF)
+
+    def z_two_away():
         arrived("MZ20")
         relay("MZ20")
 
-    chunk(3, {3: third})
-    arrived("O13", "O31", "OZ10", "OZ30", "O21", "O23")
-
-    def fourth():
-        arrived("MZ13", "MZ31")
-        relay("MZ13", "MZ31")
-
-    def fifth():
-        arrived("MZ21", "MZ23")
-        relay("MZ21", "MZ23")
+    chunk(3, {3: corners, 4: z_two_away})
+    arrived_pair("O13", "OZ10", "O21")
+
+    def z_diagonals():
+        arrived_pair("MZ13")
+        relay("MZ13", 2)
+
+    def z_corners():
+        arrived_pair("MZ21")
+        relay("MZ21", 2)
+
+    def z_last():
         arrived_half(SLOT["Z22"])
         send(half("Z22"), half("Z22"), "Z22r", Z22_HALF, sibling, HALF)
 
-    chunk(4, {2: fourth, 4: fifth})
+    chunk(4, {3: z_diagonals, 5: z_corners})
     arrived_half(P22_HALF)
-    arrived("OZ20", "OZ13", "OZ31")
-    chunk(5)
+    arrived("OZ20")
+    arrived_pair("OZ13")
+    chunk(5, {2: z_last})
     arrived_half(Z22_HALF)
-    arrived("OZ21", "OZ23")
-    chunk(6)
-
+    arrived_pair("OZ21")
     loads[2].wait()
-    for h in range(HEADS):
-        rows = slice(h * SPAN, (h + 1) * SPAN)
-        total = jnp.sum(l_ref[rows, :], axis=1, keepdims=True)
-        mixed = (acc_ref[rows, :] / total).astype(BF16)
-        ho_ref[:, h * V:(h + 1) * V] = jnp.dot(mixed, wv_ref[h], preferred_element_type=F32).astype(BF16)
+
+    def heads_of(t):
+        for h in range(t * TILE // SPAN, (t + 1) * TILE // SPAN):
+            rows = slice(h * SPAN, (h + 1) * SPAN)
+            total = jnp.sum(l_ref[rows, :], axis=1, keepdims=True)
+            mixed = (acc_ref[rows, :] / total).astype(BF16)
+            ho_ref[:, h * V:(h + 1) * V] = jnp.dot(mixed, wv_ref[h], preferred_element_type=F32).astype(BF16)
+
+    chunk(6, after=heads_of)
     loads[3].wait()
 
-    pieces = ((0, 512), (512, 384))
+    pieces = ((0, 256), (256, 256), (512, 384))
 
     def project(zh, c, piece):
         at_col = pl.multiple_of((zh * 2 + c) * OWN_D + piece[0], 128)
@@ -296,27 +312,29 @@
         copy.start()
         return copy
 
+    far = s_ref.at[0, pl.ds(0, SPAN)]
+    near = s_ref.at[1, pl.ds(0, SPAN)]
+    count = len(pieces)
     copies_a, copies_b, copies_c = [], [], []
     for n, piece in enumerate(pieces):
         window(send_a, piece)[...] = project(1 - z_hi, 1 - core, piece).astype(BF16)
         copies_a.append(rs(window(send_a, piece), window(recv_a, piece), n, sibling))
-    far = s_ref.at[0, pl.ds(0, SPAN)]
-    near = s_ref.at[1, pl.ds(0, SPAN)]
     for piece in pieces:
         window(far, piece)[...] = project(1 - z_hi, core, piece)
     for n, piece in enumerate(pieces):
-        window(send_c, piece)[...] = project(z_hi, 1 - core, piece).astype(BF16)
         copies_a[n].wait()
         window(send_b, piece)[...] = (window(far, piece)[...] + window(recv_a, piece)[...].astype(F32)).astype(BF16)
-        copies_b.append(rs(window(send_b, piece), window(recv_b, piece), 2 + n, partner))
-        copies_c.append(rs(window(send_c, piece), window(recv_c, piece), 4 + n, sibling))
+        copies_b.append(rs(window(send_b, piece), window(recv_b, piece), count + n, partner))
+        window(send_c, piece)[...] = project(z_hi, 1 - core, piece).astype(BF16)
+    copies_c.append(rs(send_c, recv_c, 2 * count, sibling))
     for piece in pieces:
         window(near, piece)[...] = project(z_hi, core, piece)
-    for n, piece in enumerate(pieces):
-        copies_c[n].wait()
+    copies_c[0].wait()
+    for piece in pieces:
         window(near, piece)[...] = window(near, piece)[...] + window(recv_c, piece)[...].astype(F32)
-    for number, rows in sends.values():
-        pltpu.make_async_copy(slab("OWN", 0, rows), slab("OWN", 0, rows), send_sem.at[number]).wait()
+    for number, rows, count in sends.values():
+        sent = slab("OWN", 0, rows, count)
+        pltpu.make_async_copy(sent, sent, send_sem.at[number]).wait()
     for n, piece in enumerate(pieces):
         copies_b[n].wait()
         out_ref[pl.ds(*piece), :] = (window(near, piece)[...] + window(recv_b, piece)[...].astype(F32)).T.astype(BF16)
@@ -337,21 +355,21 @@
             pltpu.VMEM((HEADS * V, 4 * OWN_D), BF16),
             pltpu.VMEM((ROWS, KDIM), BF16),
             pltpu.VMEM((KDIM, BLOCKS * SPAN), BF16),
-            pltpu.VMEM((1024, C), BF16),
+            pltpu.VMEM((WIDEST, C), BF16),
             pltpu.VMEM((TILE, SPAN), F32),
             pltpu.VMEM((ROWS, 128), F32),
             pltpu.VMEM((ROWS, 128), F32),
             pltpu.VMEM((ROWS, C), F32),
-            pltpu.VMEM((2, TILE, 1024), F32),
-            pltpu.VMEM((2, TILE, 1024), BF16),
+            pltpu.VMEM((2, TILE, WIDEST), F32),
+            pltpu.VMEM((2, TILE, WIDEST), BF16),
             pltpu.VMEM((2, TILE, 128), F32),
             pltpu.VMEM((SPAN, HEADS * V), BF16),
         ] + [pltpu.VMEM((SPAN, OWN_D), BF16)] * 6 + [
             pltpu.SemaphoreType.DMA((5,)),
             pltpu.SemaphoreType.DMA((N_SEND,)),
             pltpu.SemaphoreType.DMA((N_RECV,)),
-            pltpu.SemaphoreType.DMA((6,)),
-            pltpu.SemaphoreType.DMA((6,)),
+            pltpu.SemaphoreType.DMA((7,)),
+            pltpu.SemaphoreType.DMA((7,)),
         ],
         compiler_params=pltpu.CompilerParams(
             collective_id=0, has_side_effects=True, vmem_limit_bytes=58 * 2**20

time: 55 us -> 53.8 us (0.978)
  Pallas kernels: 53.2 us -> 52 us
    pallas_call x1, Pallas kernels: 53.2 us -> 52 us  [shards(): pl.pallas_call(kernel, out_shape=jax.ShapeDtypeStruct((OWN_D, SPAN), BF16...]
where the time goes in v3:
time: 53.8 us; the launch traced here: 53.7 us
  Pallas kernels  52 us (97%)
  local copies, waits for them, and re-layouts  1.64 us (3%)
    pallas_call x1, Pallas kernels, shards(): pl.pallas_call(kernel, out_shape=jax.ShapeDtypeStruct((OWN_D, SPAN), BF16...  52 us
    unnamed x1, local copies, waits for them, and re-layouts  1.64 us

profile of v3, /device:TPU:1, one launch (start us, length us, event | category | flops | bytes accessed | tf_op | source)
XLA Modules:
  0.0 53.7 jit_solution(8486665506942729093)
XLA Ops:
  0.0 52.0 %latent_attention.1 = bf16[896,128]{1,0:T(8,128)(2,1)} custom-call(bf16[128,3072]{1,0:T(8,128)(2,1)} %q_hbm.1, bf16[576,128]{1,0:T(8,128)(2,1)} %lat_hbm.1, bf16[16,128,512]{2,1,0:T(8,128)(2,1)} %wk_hbm.1, bf16[16,512,128]{2,1,0:T(8,128)(2,1)} %wv_hbm.1, bf16[2048,3584]{1,0:T(8,128)(2,1)} %wo_hbm.1, s32[32]{0:T(128)} %order_ref.1), custom_call_target="tpu_custom_call" | custom-call | flops 19327352832 | bytes 20971520 | tf_op jit(solution)/shard_map/latent_attention/pallas_call | solution.py:346
  52.0 1.6 %copy.8 = bf16[896,128]{1,0:T(8,128)(2,1)} copy(bf16[896,128]{1,0:T(8,128)(2,1)} %latent_attention.1) | data formatting | bytes 458752

commit v4 on v3

--- a/solution.py
+++ b/solution.py
@@ -345,7 +345,7 @@
     flops = 2 * ROWS * BLOCKS * SPAN * (KDIM + C)
     return pl.pallas_call(
         kernel,
-        out_shape=jax.ShapeDtypeStruct((OWN_D, SPAN), BF16),
+        out_shape=pltpu.VMEM((OWN_D, SPAN), BF16),
         in_specs=[any_spec] * 5 + [pl.BlockSpec(memory_space=pltpu.SMEM)],
         out_specs=pl.BlockSpec(memory_space=pltpu.VMEM),
         scratch_shapes=[

time: 53.8 us -> 52.2 us (0.970)
  local copies, waits for them, and re-layouts: 1.64 us -> 0.69 us
  Pallas kernels: 52 us -> 51.4 us
    unnamed x1, local copies, waits for them, and re-layouts: 1.64 us -> 0.69 us
    pallas_call x1, Pallas kernels: 52 us -> 51.4 us  [shards(): pl.pallas_call(kernel, out_shape=pltpu.VMEM((OWN_D, SPAN), BF16), in_spec...]
where the time goes in v4:
time: 52.2 us; the launch traced here: 52.1 us
  Pallas kernels  51.4 us (98%)
  local copies, waits for them, and re-layouts  0.69 us (1%)
    pallas_call x1, Pallas kernels, shards(): pl.pallas_call(kernel, out_shape=pltpu.VMEM((OWN_D, SPAN), BF16), in_spec...  51.4 us

profile of v4, /device:TPU:1, one launch (start us, length us, event | category | flops | bytes accessed | tf_op | source)
XLA Modules:
  0.0 52.1 jit_solution(11986172231530953876)
XLA Ops:
  0.0 51.4 %latent_attention.1 = bf16[896,128]{1,0:T(8,128)(2,1)S(1)} custom-call(bf16[128,3072]{1,0:T(8,128)(2,1)} %q_hbm.1, bf16[576,128]{1,0:T(8,128)(2,1)} %lat_hbm.1, bf16[16,128,512]{2,1,0:T(8,128)(2,1)} %wk_hbm.1, bf16[16,512,128]{2,1,0:T(8,128)(2,1)} %wv_hbm.1, bf16[2048,3584]{1,0:T(8,128)(2,1)} %wo_hbm.1, s32[32]{0:T(128)} %order_ref.1), custom_call_target="tpu_custom_call" | custom-call | flops 19327352832 | bytes 20971520 | tf_op jit(solution)/shard_map/latent_attention/pallas_call | solution.py:346
  51.4 0.7 %copy.8 = bf16[896,128]{1,0:T(8,128)(2,1)} copy(bf16[896,128]{1,0:T(8,128)(2,1)S(1)} %latent_attention.1) | data formatting | bytes 458752

commit v5 on v4

--- a/solution.py
+++ b/solution.py
@@ -288,14 +288,14 @@
     def heads_of(t):
         for h in range(t * TILE // SPAN, (t + 1) * TILE // SPAN):
             rows = slice(h * SPAN, (h + 1) * SPAN)
-            total = jnp.sum(l_ref[rows, :], axis=1, keepdims=True)
-            mixed = (acc_ref[rows, :] / total).astype(BF16)
+            inverse = 1.0 / jnp.sum(l_ref[rows, :], axis=1, keepdims=True)
+            mixed = (acc_ref[rows, :] * inverse).astype(BF16)
             ho_ref[:, h * V:(h + 1) * V] = jnp.dot(mixed, wv_ref[h], preferred_element_type=F32).astype(BF16)
 
     chunk(6, after=heads_of)
     loads[3].wait()
 
-    pieces = ((0, 256), (256, 256), (512, 384))
+    pieces = ((0, 256), (256, 384), (640, 256))
 
     def project(zh, c, piece):
         at_col = pl.multiple_of((zh * 2 + c) * OWN_D + piece[0], 128)

time: 52.2 us -> 52.4 us (level)
  no operation moved by 1% of the time
where the time goes in v5:
time: 52.4 us; the launch traced here: 52.3 us
  Pallas kernels  51.6 us (98%)
  local copies, waits for them, and re-layouts  0.69 us (1%)
    pallas_call x1, Pallas kernels, shards(): pl.pallas_call(kernel, out_shape=pltpu.VMEM((OWN_D, SPAN), BF16), in_spec...  51.6 us

profile of v5, /device:TPU:1, one launch (start us, length us, event | category | flops | bytes accessed | tf_op | source)
XLA Modules:
  0.0 52.3 jit_solution(15787498168513720609)
XLA Ops:
  0.0 51.6 %latent_attention.1 = bf16[896,128]{1,0:T(8,128)(2,1)S(1)} custom-call(bf16[128,3072]{1,0:T(8,128)(2,1)} %q_hbm.1, bf16[576,128]{1,0:T(8,128)(2,1)} %lat_hbm.1, bf16[16,128,512]{2,1,0:T(8,128)(2,1)} %wk_hbm.1, bf16[16,512,128]{2,1,0:T(8,128)(2,1)} %wv_hbm.1, bf16[2048,3584]{1,0:T(8,128)(2,1)} %wo_hbm.1, s32[32]{0:T(128)} %order_ref.1), custom_call_target="tpu_custom_call" | custom-call | flops 19327352832 | bytes 20971520 | tf_op jit(solution)/shard_map/latent_attention/pallas_call | solution.py:346
  51.6 0.7 %copy.8 = bf16[896,128]{1,0:T(8,128)(2,1)} copy(bf16[896,128]{1,0:T(8,128)(2,1)S(1)} %latent_attention.1) | data formatting | bytes 458752

commit v6 on v5

--- a/solution.py
+++ b/solution.py
@@ -31,8 +31,8 @@
     ("O10", "O30", "M20", "O20"),
     ("M13", "M31", "MZ10", "MZ30"),
     ("O13", "O31", "OZ10", "OZ30", "M21", "M23", "O21", "O23"),
-    ("P22", "MZ20", "OZ20", "MZ13", "MZ31", "OZ13", "OZ31", "MZ21"),
-    ("MZ23", "OZ21", "OZ23", "Z22"),
+    ("P22", "MZ20", "OZ20", "MZ13", "MZ31", "OZ13", "OZ31", "MZ21",
+     "MZ23", "OZ21", "OZ23", "Z22"),
 )
 WIDEST = max(len(group) for group in CHUNKS) * 128
 ORDER = [name for group in CHUNKS for name in group]
@@ -276,11 +276,10 @@
         arrived_half(SLOT["Z22"])
         send(half("Z22"), half("Z22"), "Z22r", Z22_HALF, sibling, HALF)
 
-    chunk(4, {3: z_diagonals, 5: z_corners})
+    chunk(4, {3: z_diagonals, 4: z_corners, 5: z_last})
     arrived_half(P22_HALF)
     arrived("OZ20")
     arrived_pair("OZ13")
-    chunk(5, {2: z_last})
     arrived_half(Z22_HALF)
     arrived_pair("OZ21")
     loads[2].wait()
@@ -292,7 +291,7 @@
             mixed = (acc_ref[rows, :] * inverse).astype(BF16)
             ho_ref[:, h * V:(h + 1) * V] = jnp.dot(mixed, wv_ref[h], preferred_element_type=F32).astype(BF16)
 
-    chunk(6, after=heads_of)
+    chunk(5, after=heads_of)
     loads[3].wait()
 
     pieces = ((0, 256), (256, 384), (640, 256))

time: 52.4 us -> 54.1 us (1.032)
  Pallas kernels: 51.6 us -> 53.3 us
    pallas_call x1, Pallas kernels: 51.6 us -> 53.3 us  [shards(): pl.pallas_call(kernel, out_shape=pltpu.VMEM((OWN_D, SPAN), BF16), in_spec...]
where the time goes in v6:
time: 54.1 us; the launch traced here: 54 us
  Pallas kernels  53.3 us (99%)
  local copies, waits for them, and re-layouts  0.69 us (1%)
    pallas_call x1, Pallas kernels, shards(): pl.pallas_call(kernel, out_shape=pltpu.VMEM((OWN_D, SPAN), BF16), in_spec...  53.3 us

profile of v6, /device:TPU:1, one launch (start us, length us, event | category | flops | bytes accessed | tf_op | source)
XLA Modules:
  0.0 54.0 jit_solution(2379495042776791811)
XLA Ops:
  0.0 53.3 %latent_attention.1 = bf16[896,128]{1,0:T(8,128)(2,1)S(1)} custom-call(bf16[128,3072]{1,0:T(8,128)(2,1)} %q_hbm.1, bf16[576,128]{1,0:T(8,128)(2,1)} %lat_hbm.1, bf16[16,128,512]{2,1,0:T(8,128)(2,1)} %wk_hbm.1, bf16[16,512,128]{2,1,0:T(8,128)(2,1)} %wv_hbm.1, bf16[2048,3584]{1,0:T(8,128)(2,1)} %wo_hbm.1, s32[32]{0:T(128)} %order_ref.1), custom_call_target="tpu_custom_call" | custom-call | flops 19327352832 | bytes 20971520 | tf_op jit(solution)/shard_map/latent_attention/pallas_call | solution.py:345
  53.3 0.7 %copy.8 = bf16[896,128]{1,0:T(8,128)(2,1)} copy(bf16[896,128]{1,0:T(8,128)(2,1)S(1)} %latent_attention.1) | data formatting | bytes 458752
